TPU v7x, 128 devices: a whole 4x4x4 slice. The times are simulated.
128 devices in a mesh: wide: 16 (over y, x_lo, core), narrow: 8 (over z, x_hi).
Axes of the slice: x: 4 (x_hi: 2, x_lo: 2; x = x_hi * 2 + x_lo), y: 4, z: 4, core: 2. Of those that a mesh axis runs over, the one named last changes fastest.
Arguments:
- interior: bfloat16 [16384, 65536], P('wide', 'narrow'), may hold values from -0.375 to 0.375
- tile_mask: int32 [256, 1024], P('wide', 'narrow'), may hold values 0 or 1
- owner: int32 [2], replicated, may hold values from 0 to 127
- stiffness: float32 [2, 512, 65536], P(None, 'wide', 'narrow'), may hold values from -4 to 4
Outputs:
- complement: float32 [2, 512, 65536], P(None, 'wide', 'narrow')
All inputs are finite; a program needn't handle non-finite values. No bound on the sum of `tile_mask` on one device may be relied on, other than what follows from the above.
Results may differ from a plain program's by a relative error of at most 0.0003.
Values may be sent and summed in bfloat16 or wider, within the bound.
A program may use at most 192 MiB of HBM per device.

v0:
```python
import jax
import jax.numpy as jnp
from jax import lax
from jax.sharding import PartitionSpec as P

PW = 512
STEPS = 2


def from_root(block, axis, source):
    block = jnp.where(lax.axis_index(axis) == source, block, jnp.zeros_like(block))
    return lax.psum(block, axis)


def scattered(portion, width, axis):
    count = width * lax.axis_size(axis)
    return lax.psum_scatter(portion(jnp.int32(0), count), axis, scatter_dimension=0, tiled=True)


def shards(interior, tile_mask, owner, stiffness):
    rows_here, cols_here = interior.shape
    tiled = (
        interior.reshape(rows_here // 64, 64, cols_here // 64, 64)
        * tile_mask.astype(jnp.bfloat16)[:, None, :, None]
    )
    masked = tiled.reshape(rows_here, cols_here)
    row_share = stiffness.shape[1]

    def product(panel_cols):
        return lax.dot_general(
            panel_cols, masked, (((0,), (0,)), ((), ())), preferred_element_type=jnp.float32
        )

    results = []
    for step_index in range(STEPS):
        first_col = owner[step_index] * PW
        holder = first_col // cols_here
        local_cols = lax.dynamic_slice_in_dim(masked, first_col % cols_here, PW, 1)
        panel_cols = from_root(local_cols, "narrow", holder)
        summed = scattered(
            lambda begin_row, row_count, held=panel_cols: product(held), row_share, "wide"
        )
        results.append(stiffness[step_index] - summed)
    return jnp.stack(results)


def solution(mesh):
    placed = (P("wide", "narrow"), P("wide", "narrow"), P(), P(None, "wide", "narrow"))
    return jax.shard_map(
        shards, mesh=mesh, in_specs=placed, out_specs=P(None, "wide", "narrow"), check_vma=False
    )
```

profile of v0, /device:TPU:1, one launch (start us, length us, event | category | flops | bytes accessed | tf_op | source)
XLA Modules:
  0.0 587.0 jit_solution(17193319454023906639)
XLA Ops:
  6.5 0.0 all-reduce.3.cloned.1.call-start
  6.5 1.3 fusion.2
  9.1 0.7 convert_element_type.3
  9.8 11.3 %mul.25 = bf16[16,64,128,64]{3,2,1,0:T(8,128)(2,1)} broadcast(bf16[16,128]{1,0:T(8,128)(2,1)S(1)} %convert_element_type.3), dimensions={0,2} | broadcast | bytes 16781312 | tf_op jit(solution)/shard_map/mul | solution.py:23
  21.1 44.0 %mul.26 = bf16[1024,8192]{1,0:T(8,128)(2,1)} reshape(bf16[16,64,128,64]{3,2,1,0:T(8,128)(2,1)} %mul.25) | data formatting | bytes 33554432 | tf_op jit(solution)/shard_map/mul | solution.py:23
  65.1 18.2 %mul.27 = bf16[1024,8192]{1,0:T(8,128)(2,1)} multiply(bf16[1024,8192]{1,0:T(8,128)(2,1)} %param.4, bf16[1024,8192]{1,0:T(8,128)(2,1)} %mul.26) | non-fusion elementwise | flops 8388608 | bytes 50331648 | tf_op jit(solution)/shard_map/mul | solution.py:23
  83.4 4.4 dynamic-slice_select_fusion.1
  87.7 0.0 all-reduce.3.cloned.1.call-update
  87.8 0.0 reduce-scatter.3.cloned.1.call-start
  87.8 110.8 %all-reduce.3.cloned.1.call-done = (bf16[1024,512]{1,0:T(8,128)(2,1)}, bf16[1024,512]{1,0:T(8,128)(2,1)}) async-done(((bf16[1024,512]{1,0:T(8,128)(2,1)}, bf16[1024,512]{1,0:T(8,128)(2,1)}), (bf16[1024,512]{1,0:T(8,128)(2,1)}, bf16[1024,512]{1,0:T(8,128)(2,1)})) %all-reduce.3.cloned.1.call-update) | async-done | bytes 2097168 | tf_op jit(solution)/shard_map/psum | solution.py:12
  198.6 16.0 %fusion.3 = f32[512,8192]{1,0:T(8,128)} fusion(bf16[1024,512]{1,0:T(8,128)(2,1)} %get-tuple-element.6, bf16[1024,8192]{1,0:T(8,128)(2,1)} %mul.27), kind=kOutput, calls=%fused_computation.8 | convolution fusion | flops 8589934592 | bytes 34603008 | tf_op jit(solution)/shard_map/dot_general | solution.py:30
  214.6 0.0 copy-start
  214.6 0.0 reduce-scatter.3.cloned.1.call-update
  214.6 0.2 reduce-scatter.5.cloned.1.call-start
  214.8 1.0 copy-done
  215.8 15.8 %fusion.4 = f32[512,8192]{1,0:T(8,128)} fusion(bf16[1024,512]{1,0:T(8,128)(2,1)S(1)} %copy-done, bf16[1024,8192]{1,0:T(8,128)(2,1)} %mul.27), kind=kOutput, calls=%fused_computation.9 | convolution fusion | flops 8589934592 | bytes 34603008 | tf_op jit(solution)/shard_map/dot_general | solution.py:30
  231.6 0.0 copy-start.1
  231.6 0.0 reduce-scatter.5.cloned.1.call-update
  231.6 162.3 %reduce-scatter.3.cloned.1.call-done = f32[32,8192]{1,0:T(8,128)} async-done(((f32[512,8192]{1,0:T(8,128)}), f32[32,8192]{1,0:T(8,128)}) %reduce-scatter.3.cloned.1.call-update) | async-done | bytes 1048592 | tf_op jit(solution)/shard_map/reduce_scatter | solution.py:17
  393.9 183.6 %reduce-scatter.5.cloned.1.call-done = f32[32,8192]{1,0:T(8,128)} async-done(((f32[512,8192]{1,0:T(8,128)}), f32[32,8192]{1,0:T(8,128)}) %reduce-scatter.5.cloned.1.call-update) | async-done | bytes 1048592 | tf_op jit(solution)/shard_map/reduce_scatter | solution.py:17
  577.4 0.0 copy-done.1
  577.4 3.1 fusion.1
  (1 shorter events, 0.0 us)
Async XLA Ops:
  6.5 192.0 %all-reduce.3.cloned.1.call-start = ((), (), s32[]{:S(2)}) async-start(), calls=%async_computation.4 | async-start | bytes 4194304 | tf_op jit(solution)/shard_map/psum | solution.py:12
  87.8 306.1 %reduce-scatter.3.cloned.1.call-start = ((), (), s32[]{:S(2)}) async-start(), calls=%async_computation.2 | async-start | bytes 17825792 | tf_op jit(solution)/shard_map/reduce_scatter | solution.py:17
  214.6 1.2 copy-start
  214.6 362.8 %reduce-scatter.5.cloned.1.call-start = ((), (), s32[]{:S(2)}) async-start(), calls=%async_computation.3 | async-start | bytes 17825792 | tf_op jit(solution)/shard_map/reduce_scatter | solution.py:17
  231.6 345.9 %copy-start.1 = (f32[2,32,8192]{2,1,0:T(8,128)S(1)}, f32[2,32,8192]{2,1,0:T(8,128)}, u32[]{:S(2)}) copy-start(f32[2,32,8192]{2,1,0:T(8,128)} %param.7) | copy-start | bytes 6291460
Sparse Core Ops, SparseCore 0:
  87.9 110.6 all-reduce.2
  214.7 179.1 reduce-scatter.2
  396.3 181.0 reduce-scatter.4
where the time goes:
time: 589 us; the launch traced here: 587 us
  waiting for transfers between devices  457 us (78%)
  local copies, waits for them, and re-layouts  57.6 us (10%)
  matrix products  31.8 us (5%)
  other arithmetic  26.4 us (4%)
  between operations  14.4 us (2%)
    reduce_scatter x2, waiting for transfers between devices, scattered(): lax.psum_scatter(portion(jnp.int32(0), count), axis, scatter_dimension=0,...  346 us
    psum x1, waiting for transfers between devices, from_root(): return lax.psum(block, axis)  111 us
    mul x2, local copies, waits for them, and re-layouts, shards(): interior.reshape(rows_here // 64, 64, cols_here // 64, 64)  55.3 us
    dot_general x2, matrix products, product(): lax.dot_general(panel_cols, masked, (((0,), (0,)), ((), ())), preferred_e...  31.8 us
    mul x1, other arithmetic, shards(): interior.reshape(rows_here // 64, 64, cols_here // 64, 64)  18.2 us
  transfers between devices with their start and end apart: 3, of which 3 were waited for; matrix products, arithmetic and copies ran while one was open for 3% of the time, Pallas kernels for 0%

commit v1 on v0

v1 whole, which is shorter than its diff:
```python
import functools

import jax
import jax.numpy as jnp
from jax import lax
from jax.experimental import pallas as pl
from jax.experimental.pallas import tpu as pltpu
from jax.sharding import PartitionSpec as P

PW = 512
STEPS = 2
MESH = pl.DeviceIdType.MESH
CHUNKS = 8
LAG = 4
HALF = 4096
DEPTH = 1024
GROUPS = ((0, 1280, (768, 512)), (1280, 1280, (768, 512)), (2560, 1536, (768, 768)))
THIRDS = ((0, 384), (384, 384), (768, 256))
TILE = 256


def pick_kernel(owner_ref, w_ref, mask_ref, out_ref):
    step, part = pl.program_id(0), pl.program_id(1)
    own = owner_ref[step]
    held = own // 16 == lax.axis_index("narrow")
    first_tile = (own % 16) * 8
    tile = lax.broadcasted_iota(jnp.int32, (128, PW), 0)
    column = lax.broadcasted_iota(jnp.int32, (128, PW), 1)
    wanted = jnp.where(held, first_tile, -1000) + column // 64
    spread = jnp.where(tile == wanted, 1.0, 0.0).astype(jnp.bfloat16)
    rows = mask_ref[pl.ds(pl.multiple_of(part * 8, 8), 8), :].astype(jnp.float32).astype(jnp.bfloat16)
    mask = jnp.dot(rows, spread, preferred_element_type=jnp.float32).astype(jnp.bfloat16)
    masked = jnp.concatenate([w_ref[64 * i : 64 * i + 64, :] * mask[i : i + 1, :] for i in range(8)], axis=0)
    place = lax.broadcasted_iota(jnp.int32, (PW, PW), 0)
    source = lax.broadcasted_iota(jnp.int32, (PW, PW), 1)
    u, v, x = (place // 64) % 2, (place // 32) % 2, (place // 16) % 2
    y = 2 * u + (u + v) % 2
    origin = y * 128 + x * 64 + ((place // 8) % 2) * 32 + (place // 128) * 8 + place % 8
    order = jnp.where(origin == source, 1.0, 0.0).astype(jnp.bfloat16)
    turned = lax.dot_general(order, masked, (((1,), (1,)), ((), ())), preferred_element_type=jnp.float32)
    out_ref[...] = turned.astype(jnp.bfloat16).reshape(4, 8, 16, PW)


def pick(owner, interior, tile_mask):
    return pl.pallas_call(
        pick_kernel,
        out_shape=jax.ShapeDtypeStruct((CHUNKS, 8, 16, DEPTH), jnp.bfloat16),
        grid_spec=pltpu.PrefetchScalarGridSpec(
            num_scalar_prefetch=1,
            grid=(STEPS, 2),
            in_specs=[
                pl.BlockSpec((PW, PW), lambda s, k, owner: (k, owner[s] % 16)),
                pl.BlockSpec((16, 128), lambda s, k, owner: (0, 0)),
            ],
            out_specs=pl.BlockSpec((4, 8, 16, PW), lambda s, k, owner: (s, 0, 0, k)),
        ),
    )(owner, interior, tile_mask)


def coded(values):
    most = jnp.maximum(jnp.max(jnp.abs(values), axis=0, keepdims=True), 1e-30)
    codes = jnp.round(values * (32767.0 / most)).astype(jnp.int32).astype(jnp.int16)
    return codes, most * (1.0 / 32767.0)


def main_kernel(
    w_hbm, mask_ref, cand, stiff_hbm, out_ref,
    b, a, r1, r2, mask2, keep, snd1, rcv1, snd2, rcv2, snd3, rcv3, snd4, rcv4, scs, scr,
    bc_s, bc_r, ac_s, ac_r, rd_s, rd_r, rs_s, rs_r, o_s, o_r, bl_s, br_s, br_r, m_s, m_r, st_s,
):
    w, n = lax.axis_index("wide"), lax.axis_index("narrow")
    core, x, y = w % 2, (w // 2) % 2, w // 4
    z, h = n // 2, n % 2
    u = y // 2
    v = (u + y % 2) % 2

    def at(y, x, core):
        return ((y * 2 + x) * 2 + core, n)

    twin = at(y, x, 1 - core)
    dims = {"v": (v, at(y + 1 - 2 * (y % 2), x, core)), "u": (u, at(3 - y, x, core)), "x": (x, at(y, 1 - x, core))}
    orders = ("vux", "uxv", "xvu")
    za, zb, hh = (w, (z + 1 - 2 * (z % 2)) * 2 + h), (w, (3 - z) * 2 + h), (w, z * 2 + 1 - h)
    routes = ((za, zb, hh), (zb, hh, za), (hh, za, zb))

    def remote(src, dst, s, r, device):
        return pltpu.make_async_remote_copy(
            src_ref=src, dst_ref=dst, send_sem=s, recv_sem=r, device_id=device, device_id_type=MESH
        )

    barrier = pltpu.get_barrier_semaphore()
    peers = (twin, dims["v"][1], dims["u"][1], dims["x"][1], za, zb, hh)
    for peer in peers:
        pl.semaphore_signal(barrier, inc=1, device_id=peer, device_id_type=MESH)

    def local_b(i):
        first = pl.multiple_of(core * HALF + i * 1024, 1024)
        return pltpu.make_async_copy(
            w_hbm.at[:, pl.ds(first, 1024)],
            b.at[pl.ds(0, DEPTH), pl.ds(pl.multiple_of(i * 1024, 1024), 1024)],
            bl_s.at[i],
        )

    def remote_b(i):
        first = pl.multiple_of((1 - core) * HALF + i * 1024, 1024)
        return remote(
            w_hbm.at[:, pl.ds(first, 1024)],
            b.at[pl.ds(DEPTH, DEPTH), pl.ds(pl.multiple_of(i * 1024, 1024), 1024)],
            br_s.at[i], br_r.at[i], twin,
        )

    mask_copy = remote(mask_ref, mask2, m_s.at[0], m_r.at[0], twin)
    stiff_copy = pltpu.make_async_copy(stiff_hbm, out_ref, st_s.at[0])

    def spread_copy(stage, third, t):
        first, width = THIRDS[third]
        cols = pl.ds(first, width)
        src = (cand, r1, r2)[stage]
        dst = (r1, r2, a)[stage]
        return remote(
            src.at[t, :, :, cols], dst.at[t, :, :, cols],
            bc_s.at[stage, third, t], bc_r.at[stage, third, t], routes[third][stage],
        )

    def twin_a(t):
        return remote(
            a.at[t, :, :, pl.ds(0, DEPTH)], a.at[t, :, :, pl.ds(DEPTH, DEPTH)], ac_s.at[t], ac_r.at[t], twin
        )

    def sum_copy(stage, g, t):
        src = (snd1, snd2, snd3)[stage][g]
        dst = (rcv1, rcv2, rcv3)[stage][g]
        peer = dims[orders[g][stage]][1]
        return (
            remote(src.at[t], dst.at[t], rd_s.at[stage, g, t], rd_r.at[stage, g, t], peer),
            remote(
                scs[g].at[stage, t], scr[g].at[stage, t], rs_s.at[stage, g, t], rs_r.at[stage, g, t], peer
            ),
        )

    def last_copy(g, t):
        return remote(snd4[g].at[t], rcv4[g].at[t], o_s.at[g, t], o_r.at[g, t], twin)

    for i in range(4):
        local_b(i).start()
    pl.semaphore_wait(barrier, len(peers))
    mask_copy.start()

    def spread_stage(stage, t):
        for third in range(3):
            first, width = THIRDS[third]
            cols = pl.ds(first, width)
            if stage > 0:
                spread_copy(stage - 1, third, t).wait_recv()
                if stage == 1:
                    r1[t, :, :, cols] = r1[t, :, :, cols] + cand[t, :, :, cols]
                if stage == 2:
                    r2[t, :, :, cols] = r2[t, :, :, cols] + r1[t, :, :, cols]
                if stage == 3:
                    a[t, :, :, cols] = a[t, :, :, cols] + r2[t, :, :, cols]
            if stage < 3:
                spread_copy(stage, third, t).start()
        if stage == 3:
            twin_a(t).start()

    def mask_slice(i):
        local_b(i).wait()
        remote_b(i).wait_recv()
        cols = pl.ds(pl.multiple_of(i * 1024, 1024), 1024)
        tile = lax.broadcasted_iota(jnp.int32, (128, 1024), 0)
        column = lax.broadcasted_iota(jnp.int32, (128, 1024), 1)
        wanted = core * 64 + i * 16 + column // 64
        spread = jnp.where(tile == wanted, 1.0, 0.0).astype(jnp.bfloat16)
        for half, ref in enumerate((mask_ref, mask2)):
            rows = ref[...].astype(jnp.float32).astype(jnp.bfloat16)
            mask = jnp.dot(rows, spread, preferred_element_type=jnp.float32).astype(jnp.bfloat16)
            for k in range(16):
                here = pl.ds(half * DEPTH + 64 * k, 64)
                b[here, cols] = b[here, cols] * mask[k : k + 1, :]

    def product(t):
        twin_a(t).wait_recv()
        for g, (first, width, tiles) in enumerate(GROUPS):
            names = orders[g]
            mine = dims[names[0]][0]

            def block(bit, second, third):
                bits = {names[0]: bit, names[1]: second, names[2]: third}
                return a[t, bits["u"] * 4 + bits["v"] * 2 + bits["x"]]

            lhs = jnp.concatenate(
                [block(bit, j, k) for bit in (1 - mine, mine) for j in (0, 1) for k in (0, 1)], axis=0
            )
            done = 0
            for size in tiles:
                here = pl.ds(done, size)
                both = jnp.dot(lhs, b[:, pl.ds(first + done, size)], preferred_element_type=jnp.float32)
                codes, scale = coded(both[:64])
                snd1[g][t, :, :, :, here] = codes.reshape(2, 2, 16, size)
                scs[g][0, t, :, here] = scale
                keep[g][t, :, :, :, here] = both[64:].reshape(2, 2, 16, size)
                done += size
            for copy in sum_copy(0, g, t):
                copy.start()

    def second(t):
        for g, (first, width, tiles) in enumerate(GROUPS):
            mine = dims[orders[g][1]][0]
            for copy in sum_copy(0, g, t):
                copy.wait_recv()

            def total(which, here, g=g):
                return keep[g][t, which, :, :, here] + rcv1[g][t, which, :, :, here].astype(jnp.int32).astype(
                    jnp.float32
                ) * scr[g][0, t, :, here].reshape(1, 1, TILE)

            def send(j, _, g=g, mine=mine):
                here = pl.ds(pl.multiple_of(j * TILE, TILE), TILE)
                codes, scale = coded(total(1 - mine, here).reshape(32, TILE))
                snd2[g][t, :, :, here] = codes.reshape(2, 16, TILE)
                scs[g][1, t, :, here] = scale
                return 0

            lax.fori_loop(0, width // TILE, send, 0)
            for copy in sum_copy(1, g, t):
                copy.start()

            def hold(j, _, g=g, mine=mine):
                here = pl.ds(pl.multiple_of(j * TILE, TILE), TILE)
                keep[g][t, mine, :, :, here] = total(mine, here)
                return 0

            lax.fori_loop(0, width // TILE, hold, 0)

    def third(t):
        for g, (first, width, tiles) in enumerate(GROUPS):
            mine2, mine3 = dims[orders[g][1]][0], dims[orders[g][2]][0]
            for copy in sum_copy(1, g, t):
                copy.wait_recv()

            def total(which, here, g=g):
                return keep[g][t, mine2, which, :, here] + rcv2[g][t, which, :, here].astype(jnp.int32).astype(
                    jnp.float32
                ) * scr[g][1, t, :, here]

            def send(j, _, g=g, mine3=mine3):
                here = pl.ds(pl.multiple_of(j * TILE, TILE), TILE)
                codes, scale = coded(total(1 - mine3, here))
                snd3[g][t, :, here] = codes
                scs[g][2, t, :, here] = scale
                return 0

            lax.fori_loop(0, width // TILE, send, 0)
            for copy in sum_copy(2, g, t):
                copy.start()

            def hold(j, _, g=g, mine2=mine2, mine3=mine3):
                here = pl.ds(pl.multiple_of(j * TILE, TILE), TILE)
                keep[g][t, mine2, mine3, :, here] = total(mine3, here)
                return 0

            lax.fori_loop(0, width // TILE, hold, 0)

    def fourth(t):
        step, rows = t // 4, pl.ds(pl.multiple_of((t % 4) * 8, 8), 8)
        for g, (first, width, tiles) in enumerate(GROUPS):
            mine2, mine3 = dims[orders[g][1]][0], dims[orders[g][2]][0]
            for copy in sum_copy(2, g, t):
                copy.wait_recv()

            def finish(j, _, g=g, first=first, mine2=mine2, mine3=mine3):
                here = pl.ds(pl.multiple_of(j * TILE, TILE), TILE)
                got = rcv3[g][t, :, here].astype(jnp.int32).astype(jnp.float32) * scr[g][2, t, :, here]
                total = keep[g][t, mine2, mine3, :, here] + got
                low, high = total[:8], total[8:]
                snd4[g][t, :, here] = jnp.where(core == 0, high, low)
                there = pl.ds(pl.multiple_of(core * HALF + first + j * TILE, TILE), TILE)
                out_ref[step, rows, there] = out_ref[step, rows, there] - jnp.where(core == 0, low, high)
                return 0

            lax.fori_loop(0, width // TILE, finish, 0)
            last_copy(g, t).start()

    def fifth(t):
        step, rows = t // 4, pl.ds(pl.multiple_of((t % 4) * 8, 8), 8)
        for g, (first, width, tiles) in enumerate(GROUPS):
            last_copy(g, t).wait_recv()
            there = pl.ds(pl.multiple_of((1 - core) * HALF + first, TILE), width)
            out_ref[step, rows, there] = out_ref[step, rows, there] - rcv4[g][t]

    def turn(i, _):
        def during(lag, body):
            @pl.when((i >= lag) & (i < lag + CHUNKS))
            def _():
                body(i - lag)

        during(0, lambda t: spread_stage(0, t))

        @pl.when(i == 0)
        def _():
            for j in range(4):
                remote_b(j).start()
            stiff_copy.start()
            mask_copy.wait_recv()

        during(1, lambda t: spread_stage(1, t))
        during(2, lambda t: spread_stage(2, t))
        during(3, lambda t: spread_stage(3, t))

        @pl.when(i < 4)
        def _():
            mask_slice(i)

        @pl.when(i == LAG + 3)
        def _():
            stiff_copy.wait()

        during(LAG, product)
        during(LAG + 1, second)
        during(LAG + 2, third)
        during(LAG + 3, fourth)
        during(LAG + 4, fifth)
        return 0

    lax.fori_loop(0, CHUNKS + LAG + 4, turn, 0)

    mask_copy.wait_send()
    for i in range(4):
        remote_b(i).wait_send()

    def drain(t, _):
        for stage in range(3):
            for third_ in range(3):
                spread_copy(stage, third_, t).wait_send()
            for g in range(3):
                for copy in sum_copy(stage, g, t):
                    copy.wait_send()
        twin_a(t).wait_send()
        for g in range(3):
            last_copy(g, t).wait_send()
        return 0

    lax.fori_loop(0, CHUNKS, drain, 0)


def shards(interior, tile_mask, owner, stiffness):
    cand = pick(owner, interior, tile_mask)
    widths = [width for _, width, _ in GROUPS]

    def each(dtype, *lead):
        return tuple(pltpu.VMEM((*lead, width), dtype) for width in widths)

    f32, i16, bf16 = jnp.float32, jnp.int16, jnp.bfloat16
    dma = pltpu.SemaphoreType.DMA
    return pl.pallas_call(
        main_kernel,
        out_shape=jax.ShapeDtypeStruct(stiffness.shape, f32),
        in_specs=[
            pl.BlockSpec(memory_space=pl.ANY),
            pl.BlockSpec(memory_space=pltpu.VMEM),
            pl.BlockSpec(memory_space=pltpu.VMEM),
            pl.BlockSpec(memory_space=pl.ANY),
        ],
        out_specs=pl.BlockSpec(memory_space=pltpu.VMEM),
        scratch_shapes=[
            pltpu.VMEM((2 * DEPTH, HALF), bf16),
            pltpu.VMEM((CHUNKS, 8, 16, 2 * DEPTH), bf16),
            pltpu.VMEM((CHUNKS, 8, 16, DEPTH), bf16),
            pltpu.VMEM((CHUNKS, 8, 16, DEPTH), bf16),
            pltpu.VMEM((16, 128), jnp.int32),
            each(f32, CHUNKS, 2, 2, 16),
            each(i16, CHUNKS, 2, 2, 16),
            each(i16, CHUNKS, 2, 2, 16),
            each(i16, CHUNKS, 2, 16),
            each(i16, CHUNKS, 2, 16),
            each(i16, CHUNKS, 16),
            each(i16, CHUNKS, 16),
            each(f32, CHUNKS, 8),
            each(f32, CHUNKS, 8),
            each(f32, 3, CHUNKS, 1),
            each(f32, 3, CHUNKS, 1),
            dma((3, 3, CHUNKS)), dma((3, 3, CHUNKS)),
            dma((CHUNKS,)), dma((CHUNKS,)),
            dma((3, 3, CHUNKS)), dma((3, 3, CHUNKS)),
            dma((3, 3, CHUNKS)), dma((3, 3, CHUNKS)),
            dma((3, CHUNKS)), dma((3, CHUNKS)),
            dma((4,)), dma((4,)), dma((4,)),
            dma((1,)), dma((1,)), dma((1,)),
        ],
        compiler_params=pltpu.CompilerParams(
            collective_id=0, has_side_effects=True, vmem_limit_bytes=62 * 1024 * 1024
        ),
    )(interior, tile_mask, cand, stiffness)


def solution(mesh):
    placed = (P("wide", "narrow"), P("wide", "narrow"), P(), P(None, "wide", "narrow"))
    return jax.shard_map(
        shards, mesh=mesh, in_specs=placed, out_specs=P(None, "wide", "narrow"), check_vma=False
    )
```

time: 589 us -> 138 us (0.23)
  waiting for transfers between devices: 457 us -> 0 us
  Pallas kernels: 0 us -> 134 us
  local copies, waits for them, and re-layouts: 57.6 us -> 3.06 us
  matrix products: 31.8 us -> 0 us
  other arithmetic: 26.4 us -> 0 us
  between operations: 14.4 us -> 0.01 us
    reduce_scatter x2 -> x0, waiting for transfers between devices: 346 us -> none  [scattered(): lax.psum_scatter(portion(jnp.int32(0), count), axis, scatter_dimension=0,...]
    pallas_call x0 -> x2, Pallas kernels: none -> 134 us  [the longest x1 128 us: shards(): pl.pallas_call(main_kernel, out_shape=jax.ShapeDtypeStruct(stiffness.shap...]
    psum x1 -> x0, waiting for transfers between devices: 111 us -> none  [from_root(): return lax.psum(block, axis)]
    mul x2 -> x0, local copies, waits for them, and re-layouts: 55.3 us -> none  [shards(): interior.reshape(rows_here // 64, 64, cols_here // 64, 64)]
    dot_general x2 -> x0, matrix products: 31.8 us -> none  [product(): lax.dot_general(panel_cols, masked, (((0,), (0,)), ((), ())), preferred_e...]
    mul x1 -> x0, other arithmetic: 18.2 us -> none  [shards(): interior.reshape(rows_here // 64, 64, cols_here // 64, 64)]
  transfers between devices with their start and end apart: 3 -> 0, of which waited for: 3 -> 0; matrix products, arithmetic and copies ran while one was open for 3% -> 0% of each run, Pallas kernels for 0% -> 0%
where the time goes in v1:
time: 138 us; the launch traced here: 137 us
  Pallas kernels  134 us (97%)
  local copies, waits for them, and re-layouts  3.06 us (2%)
    pallas_call x1, Pallas kernels, shards(): pl.pallas_call(main_kernel, out_shape=jax.ShapeDtypeStruct(stiffness.shap...  128 us
    pallas_call x1, Pallas kernels, pick(): pl.pallas_call(pick_kernel, out_shape=jax.ShapeDtypeStruct((CHUNKS, 8, 16...  6.25 us
    unnamed x1, local copies, waits for them, and re-layouts  3.06 us

profile of v1, /device:TPU:1, one launch (start us, length us, event | category | flops | bytes accessed | tf_op | source)
XLA Modules:
  0.0 137.3 jit_solution(5600088565391052798)
XLA Ops:
  0.0 6.3 %shard_map.46.cand = bf16[8,8,16,1024]{3,2,1,0:T(8,128)(2,1)} custom-call(s32[2]{0:T(128)} %owner_ref.1, bf16[1024,8192]{1,0:T(8,128)(2,1)} %w_hbm.1, s32[16,128]{1,0:T(8,128)} %mask_ref.3), custom_call_target="tpu_custom_call" | custom-call | tf_op jit(solution)/shard_map/pallas_call | solution.py:45
  6.3 128.0 %shard_map.47 = f32[2,32,8192]{2,1,0:T(8,128)} custom-call(bf16[1024,8192]{1,0:T(8,128)(2,1)} %w_hbm.1, s32[16,128]{1,0:T(8,128)} %mask_ref.3, bf16[8,8,16,1024]{3,2,1,0:T(8,128)(2,1)} %shard_map.46.cand, f32[2,32,8192]{2,1,0:T(8,128)} %stiff_hbm.1), custom_call_target="tpu_custom_call" | custom-call | tf_op jit(solution)/shard_map/pallas_call | solution.py:355
  134.3 3.1 %copy.6 = f32[2,32,8192]{2,1,0:T(8,128)} copy(f32[2,32,8192]{2,1,0:T(8,128)} %shard_map.47) | data formatting | bytes 4194304

commit v2 on v1

--- a/solution.py
+++ b/solution.py
@@ -11,15 +11,15 @@
 STEPS = 2
 MESH = pl.DeviceIdType.MESH
 CHUNKS = 8
+SLOTS = 4
 LAG = 4
 HALF = 4096
 DEPTH = 1024
-GROUPS = ((0, 1280, (768, 512)), (1280, 1280, (768, 512)), (2560, 1536, (768, 768)))
-THIRDS = ((0, 384), (384, 384), (768, 256))
+GROUPS = ((0, 1792, (768, 512, 512)), (1792, 1536, (768, 768)), (3328, 768, (768,)))
 TILE = 256
 
 
-def pick_kernel(owner_ref, w_ref, mask_ref, out_ref):
+def pick_kernel(owner_ref, w_ref, mask_ref, out_ref, order):
     step, part = pl.program_id(0), pl.program_id(1)
     own = owner_ref[step]
     held = own // 16 == lax.axis_index("narrow")
@@ -29,15 +29,22 @@
     wanted = jnp.where(held, first_tile, -1000) + column // 64
     spread = jnp.where(tile == wanted, 1.0, 0.0).astype(jnp.bfloat16)
     rows = mask_ref[pl.ds(pl.multiple_of(part * 8, 8), 8), :].astype(jnp.float32).astype(jnp.bfloat16)
-    mask = jnp.dot(rows, spread, preferred_element_type=jnp.float32).astype(jnp.bfloat16)
-    masked = jnp.concatenate([w_ref[64 * i : 64 * i + 64, :] * mask[i : i + 1, :] for i in range(8)], axis=0)
-    place = lax.broadcasted_iota(jnp.int32, (PW, PW), 0)
-    source = lax.broadcasted_iota(jnp.int32, (PW, PW), 1)
-    u, v, x = (place // 64) % 2, (place // 32) % 2, (place // 16) % 2
-    y = 2 * u + (u + v) % 2
-    origin = y * 128 + x * 64 + ((place // 8) % 2) * 32 + (place // 128) * 8 + place % 8
-    order = jnp.where(origin == source, 1.0, 0.0).astype(jnp.bfloat16)
-    turned = lax.dot_general(order, masked, (((1,), (1,)), ((), ())), preferred_element_type=jnp.float32)
+    mask = jnp.dot(rows, spread, preferred_element_type=jnp.float32)
+    pieces = []
+    for i in range(8):
+        factor = jnp.broadcast_to(mask[i : i + 1, :], (16, PW)).astype(jnp.bfloat16)
+        pieces += [w_ref[k : k + 16, :] * factor for k in range(64 * i, 64 * i + 64, 16)]
+    masked = jnp.concatenate(pieces, axis=0)
+    @pl.when((step == 0) & (part == 0))
+    def _():
+        place = lax.broadcasted_iota(jnp.int32, (PW, 1), 0)
+        source = lax.broadcasted_iota(jnp.int32, (PW, PW), 1)
+        u, v, x = (place // 64) % 2, (place // 32) % 2, (place // 16) % 2
+        y = 2 * u + (u + v) % 2
+        origin = y * 128 + x * 64 + ((place // 8) % 2) * 32 + (place // 128) * 8 + place % 8
+        order[...] = jnp.where(origin == source, 1.0, 0.0).astype(jnp.bfloat16)
+
+    turned = lax.dot_general(order[...], masked, (((1,), (1,)), ((), ())), preferred_element_type=jnp.float32)
     out_ref[...] = turned.astype(jnp.bfloat16).reshape(4, 8, 16, PW)
 
 
@@ -53,6 +60,7 @@
                 pl.BlockSpec((16, 128), lambda s, k, owner: (0, 0)),
             ],
             out_specs=pl.BlockSpec((4, 8, 16, PW), lambda s, k, owner: (s, 0, 0, k)),
+            scratch_shapes=[pltpu.VMEM((PW, PW), jnp.bfloat16)],
         ),
     )(owner, interior, tile_mask)
 
@@ -64,9 +72,9 @@
 
 
 def main_kernel(
-    w_hbm, mask_ref, cand, stiff_hbm, out_ref,
-    b, a, r1, r2, mask2, keep, snd1, rcv1, snd2, rcv2, snd3, rcv3, snd4, rcv4, scs, scr,
-    bc_s, bc_r, ac_s, ac_r, rd_s, rd_r, rs_s, rs_r, o_s, o_r, bl_s, br_s, br_r, m_s, m_r, st_s,
+    w_hbm, mask_ref, cand, stiff_hbm, out_hbm,
+    out_ref, mine_c, b, a, r1, s1, r2, mask2, keep, snd1, rcv1, snd2, rcv2, snd3, rcv3, snd4, rcv4, scs, scr,
+    c1_s, c1_r, c2_s, c2_r, c3_s, c3_r, ac_s, ac_r, rd_s, rd_r, rs_s, rs_r, o_s, o_r, bl_s, br_s, br_r, m_s, m_r, st_s, mc_s, w_s,
 ):
     w, n = lax.axis_index("wide"), lax.axis_index("narrow")
     core, x, y = w % 2, (w // 2) % 2, w // 4
@@ -80,8 +88,9 @@
     twin = at(y, x, 1 - core)
     dims = {"v": (v, at(y + 1 - 2 * (y % 2), x, core)), "u": (u, at(3 - y, x, core)), "x": (x, at(y, 1 - x, core))}
     orders = ("vux", "uxv", "xvu")
-    za, zb, hh = (w, (z + 1 - 2 * (z % 2)) * 2 + h), (w, (3 - z) * 2 + h), (w, z * 2 + 1 - h)
-    routes = ((za, zb, hh), (zb, hh, za), (hh, za, zb))
+    others = [(z + d) % 4 for d in (1, 2, 3)]
+    ring = [(w, other * 2 + h) for other in others]
+    across = (w, z * 2 + 1 - h)
 
     def remote(src, dst, s, r, device):
         return pltpu.make_async_remote_copy(
@@ -89,7 +98,7 @@
         )
 
     barrier = pltpu.get_barrier_semaphore()
-    peers = (twin, dims["v"][1], dims["u"][1], dims["x"][1], za, zb, hh)
+    peers = (twin, dims["v"][1], dims["u"][1], dims["x"][1], *ring, across)
     for peer in peers:
         pl.semaphore_signal(barrier, inc=1, device_id=peer, device_id_type=MESH)
 
@@ -111,82 +120,113 @@
 
     mask_copy = remote(mask_ref, mask2, m_s.at[0], m_r.at[0], twin)
     stiff_copy = pltpu.make_async_copy(stiff_hbm, out_ref, st_s.at[0])
-
-    def spread_copy(stage, third, t):
-        first, width = THIRDS[third]
-        cols = pl.ds(first, width)
-        src = (cand, r1, r2)[stage]
-        dst = (r1, r2, a)[stage]
-        return remote(
-            src.at[t, :, :, cols], dst.at[t, :, :, cols],
-            bc_s.at[stage, third, t], bc_r.at[stage, third, t], routes[third][stage],
-        )
+    mine_copy = pltpu.make_async_copy(cand.at[:, pl.ds(2 * z, 2)], mine_c, mc_s.at[0])
+
+    def out_copy(t):
+        rows = pl.ds(pl.multiple_of((t % 4) * 8, 8), 8)
+        return pltpu.make_async_copy(out_ref.at[t // 4, rows], out_hbm.at[t // 4, rows], w_s.at[t])
+
+
+    def quarter(z):
+        return pl.ds(2 * z, 2)
+
+    def scatter(d, t):
+        return remote(cand.at[t, quarter(others[d])], r1.at[t, d], c1_s.at[d, t % SLOTS], c1_r.at[d, t % SLOTS], ring[d])
+
+    def cross(t):
+        return remote(s1.at[t], r2.at[t], c2_s.at[t % SLOTS], c2_r.at[t % SLOTS], across)
+
+    def gather(d, t):
+        piece = a.at[t, 0, quarter(z)]
+        return remote(piece, piece, c3_s.at[d, t % SLOTS], c3_r.at[d, t % SLOTS], ring[d])
 
     def twin_a(t):
-        return remote(
-            a.at[t, :, :, pl.ds(0, DEPTH)], a.at[t, :, :, pl.ds(DEPTH, DEPTH)], ac_s.at[t], ac_r.at[t], twin
-        )
+        return remote(a.at[t, 0], a.at[t, 1], ac_s.at[t % SLOTS], ac_r.at[t % SLOTS], twin)
 
     def sum_copy(stage, g, t):
         src = (snd1, snd2, snd3)[stage][g]
         dst = (rcv1, rcv2, rcv3)[stage][g]
         peer = dims[orders[g][stage]][1]
+        slot = t % SLOTS
         return (
-            remote(src.at[t], dst.at[t], rd_s.at[stage, g, t], rd_r.at[stage, g, t], peer),
-            remote(
-                scs[g].at[stage, t], scr[g].at[stage, t], rs_s.at[stage, g, t], rs_r.at[stage, g, t], peer
-            ),
+            remote(src.at[t], dst.at[t], rd_s.at[stage, g, slot], rd_r.at[stage, g, slot], peer),
+            remote(scs[g].at[stage, t], scr[g].at[stage, t], rs_s.at[stage, g, slot], rs_r.at[stage, g, slot], peer),
         )
 
     def last_copy(g, t):
-        return remote(snd4[g].at[t], rcv4[g].at[t], o_s.at[g, t], o_r.at[g, t], twin)
-
+        return remote(snd4[g].at[t], rcv4[g].at[t], o_s.at[g, t % SLOTS], o_r.at[g, t % SLOTS], twin)
+
+    mine_copy.start()
     for i in range(4):
         local_b(i).start()
     pl.semaphore_wait(barrier, len(peers))
     mask_copy.start()
 
-    def spread_stage(stage, t):
-        for third in range(3):
-            first, width = THIRDS[third]
-            cols = pl.ds(first, width)
-            if stage > 0:
-                spread_copy(stage - 1, third, t).wait_recv()
-                if stage == 1:
-                    r1[t, :, :, cols] = r1[t, :, :, cols] + cand[t, :, :, cols]
-                if stage == 2:
-                    r2[t, :, :, cols] = r2[t, :, :, cols] + r1[t, :, :, cols]
-                if stage == 3:
-                    a[t, :, :, cols] = a[t, :, :, cols] + r2[t, :, :, cols]
-            if stage < 3:
-                spread_copy(stage, third, t).start()
-        if stage == 3:
-            twin_a(t).start()
-
-    def mask_slice(i):
-        local_b(i).wait()
-        remote_b(i).wait_recv()
+    def launch(t, copies):
+        @pl.when(t >= SLOTS)
+        def _():
+            for copy in copies(t - SLOTS):
+                copy.wait_send()
+
+        for copy in copies(t):
+            copy.start()
+
+    def scatters(t):
+        return [scatter(d, t) for d in range(3)]
+
+    def gathers(t):
+        return [gather(d, t) for d in range(3)]
+
+    def spread_0(t):
+        launch(t, scatters)
+
+    def spread_1(t):
+        for copy in scatters(t):
+            copy.wait_recv()
+        s1[t] = (mine_c[t] + r1[t, 0]) + (r1[t, 1] + r1[t, 2])
+        launch(t, lambda t: [cross(t)])
+
+    def spread_2(t):
+        cross(t).wait_recv()
+        a[t, 0, quarter(z)] = s1[t] + r2[t]
+        launch(t, gathers)
+
+    def spread_3(t):
+        for copy in gathers(t):
+            copy.wait_recv()
+        launch(t, lambda t: [twin_a(t)])
+
+    def mask_slice(half, ref, i):
         cols = pl.ds(pl.multiple_of(i * 1024, 1024), 1024)
         tile = lax.broadcasted_iota(jnp.int32, (128, 1024), 0)
-        column = lax.broadcasted_iota(jnp.int32, (128, 1024), 1)
+        column = lax.broadcasted_iota(jnp.int32, (1, 1024), 1)
         wanted = core * 64 + i * 16 + column // 64
         spread = jnp.where(tile == wanted, 1.0, 0.0).astype(jnp.bfloat16)
-        for half, ref in enumerate((mask_ref, mask2)):
-            rows = ref[...].astype(jnp.float32).astype(jnp.bfloat16)
-            mask = jnp.dot(rows, spread, preferred_element_type=jnp.float32).astype(jnp.bfloat16)
-            for k in range(16):
-                here = pl.ds(half * DEPTH + 64 * k, 64)
-                b[here, cols] = b[here, cols] * mask[k : k + 1, :]
+        rows = ref[...].astype(jnp.float32).astype(jnp.bfloat16)
+        mask = jnp.dot(rows, spread, preferred_element_type=jnp.float32)
+        for k in range(16):
+            factor = jnp.broadcast_to(mask[k : k + 1, :], (16, 1024)).astype(jnp.bfloat16)
+            for row in range(half * DEPTH + 64 * k, half * DEPTH + 64 * k + 64, 16):
+                b[row : row + 16, cols] = b[row : row + 16, cols] * factor
 
     def product(t):
         twin_a(t).wait_recv()
         for g, (first, width, tiles) in enumerate(GROUPS):
+            if g == 1:
+
+                @pl.when(t == 0)
+                def _():
+                    for j in (2, 3):
+                        remote_b(j).wait_recv()
+                        mask_slice(1, mask2, j)
+
             names = orders[g]
             mine = dims[names[0]][0]
 
             def block(bit, second, third):
                 bits = {names[0]: bit, names[1]: second, names[2]: third}
-                return a[t, bits["u"] * 4 + bits["v"] * 2 + bits["x"]]
+                index = bits["u"] * 4 + bits["v"] * 2 + bits["x"]
+                return jnp.concatenate([a[t, 0, index], a[t, 1, index]], axis=1)
 
             lhs = jnp.concatenate(
                 [block(bit, j, k) for bit in (1 - mine, mine) for j in (0, 1) for k in (0, 1)], axis=0
@@ -200,8 +240,7 @@
                 scs[g][0, t, :, here] = scale
                 keep[g][t, :, :, :, here] = both[64:].reshape(2, 2, 16, size)
                 done += size
-            for copy in sum_copy(0, g, t):
-                copy.start()
+            launch(t, functools.partial(sum_copy, 0, g))
 
     def second(t):
         for g, (first, width, tiles) in enumerate(GROUPS):
@@ -222,8 +261,7 @@
                 return 0
 
             lax.fori_loop(0, width // TILE, send, 0)
-            for copy in sum_copy(1, g, t):
-                copy.start()
+            launch(t, functools.partial(sum_copy, 1, g))
 
             def hold(j, _, g=g, mine=mine):
                 here = pl.ds(pl.multiple_of(j * TILE, TILE), TILE)
@@ -251,8 +289,7 @@
                 return 0
 
             lax.fori_loop(0, width // TILE, send, 0)
-            for copy in sum_copy(2, g, t):
-                copy.start()
+            launch(t, functools.partial(sum_copy, 2, g))
 
             def hold(j, _, g=g, mine2=mine2, mine3=mine3):
                 here = pl.ds(pl.multiple_of(j * TILE, TILE), TILE)
@@ -279,7 +316,7 @@
                 return 0
 
             lax.fori_loop(0, width // TILE, finish, 0)
-            last_copy(g, t).start()
+            launch(t, lambda t, g=g: [last_copy(g, t)])
 
     def fifth(t):
         step, rows = t // 4, pl.ds(pl.multiple_of((t % 4) * 8, 8), 8)
@@ -287,6 +324,7 @@
             last_copy(g, t).wait_recv()
             there = pl.ds(pl.multiple_of((1 - core) * HALF + first, TILE), width)
             out_ref[step, rows, there] = out_ref[step, rows, there] - rcv4[g][t]
+        out_copy(t).start()
 
     def turn(i, _):
         def during(lag, body):
@@ -294,28 +332,46 @@
             def _():
                 body(i - lag)
 
-        during(0, lambda t: spread_stage(0, t))
+        @pl.when(i < LAG)
+        def _():
+            during(3, spread_3)
+            during(2, spread_2)
+            during(1, spread_1)
+            during(0, spread_0)
 
         @pl.when(i == 0)
         def _():
             for j in range(4):
                 remote_b(j).start()
             stiff_copy.start()
+            mine_copy.wait()
             mask_copy.wait_recv()
 
-        during(1, lambda t: spread_stage(1, t))
-        during(2, lambda t: spread_stage(2, t))
-        during(3, lambda t: spread_stage(3, t))
-
-        @pl.when(i < 4)
-        def _():
-            mask_slice(i)
+        @pl.when(i < 2)
+        def _():
+            for j in range(2):
+                local_b(2 * i + j).wait()
+                mask_slice(0, mask_ref, 2 * i + j)
+
+        @pl.when(i == 3)
+        def _():
+            for j in range(2):
+                remote_b(j).wait_recv()
+                mask_slice(1, mask2, j)
+
+        during(LAG, product)
+
+        @pl.when(i >= LAG)
+        def _():
+            during(0, spread_0)
+            during(1, spread_1)
+            during(2, spread_2)
+            during(3, spread_3)
 
         @pl.when(i == LAG + 3)
         def _():
             stiff_copy.wait()
 
-        during(LAG, product)
         during(LAG + 1, second)
         during(LAG + 2, third)
         during(LAG + 3, fourth)
@@ -328,19 +384,27 @@
     for i in range(4):
         remote_b(i).wait_send()
 
+    def written(t, _):
+        out_copy(t).wait()
+        return 0
+
+    lax.fori_loop(0, CHUNKS, written, 0)
+
     def drain(t, _):
         for stage in range(3):
-            for third_ in range(3):
-                spread_copy(stage, third_, t).wait_send()
             for g in range(3):
                 for copy in sum_copy(stage, g, t):
                     copy.wait_send()
+        for d in range(3):
+            scatter(d, t).wait_send()
+            gather(d, t).wait_send()
+        cross(t).wait_send()
         twin_a(t).wait_send()
         for g in range(3):
             last_copy(g, t).wait_send()
         return 0
 
-    lax.fori_loop(0, CHUNKS, drain, 0)
+    lax.fori_loop(CHUNKS - SLOTS, CHUNKS, drain, 0)
 
 
 def shards(interior, tile_mask, owner, stiffness):
@@ -358,15 +422,18 @@
         in_specs=[
             pl.BlockSpec(memory_space=pl.ANY),
             pl.BlockSpec(memory_space=pltpu.VMEM),
-            pl.BlockSpec(memory_space=pltpu.VMEM),
+            pl.BlockSpec(memory_space=pl.ANY),
             pl.BlockSpec(memory_space=pl.ANY),
         ],
-        out_specs=pl.BlockSpec(memory_space=pltpu.VMEM),
+        out_specs=pl.BlockSpec(memory_space=pl.ANY),
         scratch_shapes=[
+            pltpu.VMEM((STEPS, 32, 2 * HALF), f32),
+            pltpu.VMEM((CHUNKS, 2, 16, DEPTH), bf16),
             pltpu.VMEM((2 * DEPTH, HALF), bf16),
-            pltpu.VMEM((CHUNKS, 8, 16, 2 * DEPTH), bf16),
-            pltpu.VMEM((CHUNKS, 8, 16, DEPTH), bf16),
-            pltpu.VMEM((CHUNKS, 8, 16, DEPTH), bf16),
+            pltpu.VMEM((CHUNKS, 2, 8, 16, DEPTH), bf16),
+            pltpu.VMEM((CHUNKS, 3, 2, 16, DEPTH), bf16),
+            pltpu.VMEM((CHUNKS, 2, 16, DEPTH), bf16),
+            pltpu.VMEM((CHUNKS, 2, 16, DEPTH), bf16),
             pltpu.VMEM((16, 128), jnp.int32),
             each(f32, CHUNKS, 2, 2, 16),
             each(i16, CHUNKS, 2, 2, 16),
@@ -379,13 +446,13 @@
             each(f32, CHUNKS, 8),
             each(f32, 3, CHUNKS, 1),
             each(f32, 3, CHUNKS, 1),
-            dma((3, 3, CHUNKS)), dma((3, 3, CHUNKS)),
-            dma((CHUNKS,)), dma((CHUNKS,)),
-            dma((3, 3, CHUNKS)), dma((3, 3, CHUNKS)),
-            dma((3, 3, CHUNKS)), dma((3, 3, CHUNKS)),
-            dma((3, CHUNKS)), dma((3, CHUNKS)),
+            dma((3, SLOTS)), dma((3, SLOTS)), dma((SLOTS,)), dma((SLOTS,)), dma((3, SLOTS)), dma((3, SLOTS)),
+            dma((SLOTS,)), dma((SLOTS,)),
+            dma((3, 3, SLOTS)), dma((3, 3, SLOTS)),
+            dma((3, 3, SLOTS)), dma((3, 3, SLOTS)),
+            dma((3, SLOTS)), dma((3, SLOTS)),
             dma((4,)), dma((4,)), dma((4,)),
-            dma((1,)), dma((1,)), dma((1,)),
+            dma((1,)), dma((1,)), dma((1,)), dma((1,)), dma((CHUNKS,)),
         ],
         compiler_params=pltpu.CompilerParams(
             collective_id=0, has_side_effects=True, vmem_limit_bytes=62 * 1024 * 1024

time: 138 us -> 109 us (0.79)
  Pallas kernels: 134 us -> 106 us
    pallas_call x1, Pallas kernels: 128 us -> 99.9 us  [shards(): pl.pallas_call(main_kernel, out_shape=jax.ShapeDtypeStruct(stiffness.shap...]
where the time goes in v2:
time: 109 us
  Pallas kernels  106 us (97%)
  local copies, waits for them, and re-layouts  3.06 us (3%)
    pallas_call x1, Pallas kernels, shards(): pl.pallas_call(main_kernel, out_shape=jax.ShapeDtypeStruct(stiffness.shap...  99.9 us
    pallas_call x1, Pallas kernels, pick(): pl.pallas_call(pick_kernel, out_shape=jax.ShapeDtypeStruct((CHUNKS, 8, 16...  6.2 us
    unnamed x1, local copies, waits for them, and re-layouts  3.06 us

profile of v2, /device:TPU:1, one launch (start us, length us, event | category | flops | bytes accessed | tf_op | source)
XLA Modules:
  0.0 109.1 jit_solution(9690299500184396847)
XLA Ops:
  0.0 6.2 %shard_map.46.cand = bf16[8,8,16,1024]{3,2,1,0:T(8,128)(2,1)} custom-call(s32[2]{0:T(128)} %owner_ref.1, bf16[1024,8192]{1,0:T(8,128)(2,1)} %w_hbm.1, s32[16,128]{1,0:T(8,128)} %mask_ref.3), custom_call_target="tpu_custom_call" | custom-call | tf_op jit(solution)/shard_map/pallas_call | solution.py:52
  6.2 99.9 %shard_map.47 = f32[2,32,8192]{2,1,0:T(8,128)} custom-call(bf16[1024,8192]{1,0:T(8,128)(2,1)} %w_hbm.1, s32[16,128]{1,0:T(8,128)} %mask_ref.3, bf16[8,8,16,1024]{3,2,1,0:T(8,128)(2,1)} %shard_map.46.cand, f32[2,32,8192]{2,1,0:T(8,128)} %stiff_hbm.1), custom_call_target="tpu_custom_call" | custom-call | tf_op jit(solution)/shard_map/pallas_call | solution.py:419
  106.1 3.1 %copy.6 = f32[2,32,8192]{2,1,0:T(8,128)} copy(f32[2,32,8192]{2,1,0:T(8,128)} %shard_map.47) | data formatting | bytes 4194304

commit v3 on v2

--- a/solution.py
+++ b/solution.py
@@ -15,54 +15,109 @@
 LAG = 4
 HALF = 4096
 DEPTH = 1024
-GROUPS = ((0, 1792, (768, 512, 512)), (1792, 1536, (768, 768)), (3328, 768, (768,)))
-TILE = 256
-
-
-def pick_kernel(owner_ref, w_ref, mask_ref, out_ref, order):
-    step, part = pl.program_id(0), pl.program_id(1)
-    own = owner_ref[step]
-    held = own // 16 == lax.axis_index("narrow")
-    first_tile = (own % 16) * 8
+GROUPS = ((0, 1792, (1024, 768)), (1792, 1408, (768, 640)), (3200, 896, (896,)))
+TILES = (256, 128, 128)
+
+
+def pick_kernel(owner_ref, w_hbm, mask_ref, out_hbm, order, blocks, turned, in_sem, out_sem):
+    parts = [(step, part) for step in range(STEPS) for part in range(2)]
+
+    def fetch(step, part):
+        first = pl.multiple_of(owner_ref[step] % 16 * PW, PW)
+        here = 2 * step + part
+        return pltpu.make_async_copy(
+            w_hbm.at[pl.ds(part * PW, PW), pl.ds(first, PW)], blocks.at[here], in_sem.at[here]
+        )
+
+    def leave(step, part):
+        here = 2 * step + part
+        return pltpu.make_async_copy(
+            turned.at[here], out_hbm.at[pl.ds(4 * step, 4), :, :, pl.ds(part * PW, PW)], out_sem.at[here]
+        )
+
+    for step, part in parts:
+        fetch(step, part).start()
+    place = lax.broadcasted_iota(jnp.int32, (PW, 1), 0)
+    source = lax.broadcasted_iota(jnp.int32, (PW, PW), 1)
+    u, v, x = (place // 64) % 2, (place // 32) % 2, (place // 16) % 2
+    y = 2 * u + (u + v) % 2
+    origin = y * 128 + x * 64 + ((place // 8) % 2) * 32 + (place // 128) * 8 + place % 8
+    order[...] = jnp.where(origin == source, 1.0, 0.0).astype(jnp.bfloat16)
     tile = lax.broadcasted_iota(jnp.int32, (128, PW), 0)
-    column = lax.broadcasted_iota(jnp.int32, (128, PW), 1)
-    wanted = jnp.where(held, first_tile, -1000) + column // 64
-    spread = jnp.where(tile == wanted, 1.0, 0.0).astype(jnp.bfloat16)
-    rows = mask_ref[pl.ds(pl.multiple_of(part * 8, 8), 8), :].astype(jnp.float32).astype(jnp.bfloat16)
-    mask = jnp.dot(rows, spread, preferred_element_type=jnp.float32)
-    pieces = []
-    for i in range(8):
-        factor = jnp.broadcast_to(mask[i : i + 1, :], (16, PW)).astype(jnp.bfloat16)
-        pieces += [w_ref[k : k + 16, :] * factor for k in range(64 * i, 64 * i + 64, 16)]
-    masked = jnp.concatenate(pieces, axis=0)
-    @pl.when((step == 0) & (part == 0))
-    def _():
-        place = lax.broadcasted_iota(jnp.int32, (PW, 1), 0)
-        source = lax.broadcasted_iota(jnp.int32, (PW, PW), 1)
-        u, v, x = (place // 64) % 2, (place // 32) % 2, (place // 16) % 2
-        y = 2 * u + (u + v) % 2
-        origin = y * 128 + x * 64 + ((place // 8) % 2) * 32 + (place // 128) * 8 + place % 8
-        order[...] = jnp.where(origin == source, 1.0, 0.0).astype(jnp.bfloat16)
-
-    turned = lax.dot_general(order[...], masked, (((1,), (1,)), ((), ())), preferred_element_type=jnp.float32)
-    out_ref[...] = turned.astype(jnp.bfloat16).reshape(4, 8, 16, PW)
+    column = lax.broadcasted_iota(jnp.int32, (1, PW), 1)
+    rows = mask_ref[...].astype(jnp.float32).astype(jnp.bfloat16)
+    for step in range(STEPS):
+        own = owner_ref[step]
+        held = own // 16 == lax.axis_index("narrow")
+        wanted = jnp.where(held, (own % 16) * 8, -1000) + column // 64
+        spread = jnp.where(tile == wanted, 1.0, 0.0).astype(jnp.bfloat16)
+        mask = jnp.dot(rows, spread, preferred_element_type=jnp.float32)
+        for part in range(2):
+            here = 2 * step + part
+            fetch(step, part).wait()
+            pieces = []
+            for i in range(8):
+                row = 8 * part + i
+                factor = jnp.broadcast_to(mask[row : row + 1, :], (16, PW)).astype(jnp.bfloat16)
+                pieces += [blocks[here, k : k + 16, :] * factor for k in range(64 * i, 64 * i + 64, 16)]
+            masked = jnp.concatenate(pieces, axis=0)
+            product = lax.dot_general(
+                order[...], masked, (((1,), (1,)), ((), ())), preferred_element_type=jnp.float32
+            )
+            turned[here] = product.astype(jnp.bfloat16).reshape(4, 8, 16, PW)
+            leave(step, part).start()
+    for step, part in parts:
+        leave(step, part).wait()
 
 
 def pick(owner, interior, tile_mask):
     return pl.pallas_call(
         pick_kernel,
         out_shape=jax.ShapeDtypeStruct((CHUNKS, 8, 16, DEPTH), jnp.bfloat16),
-        grid_spec=pltpu.PrefetchScalarGridSpec(
-            num_scalar_prefetch=1,
-            grid=(STEPS, 2),
-            in_specs=[
-                pl.BlockSpec((PW, PW), lambda s, k, owner: (k, owner[s] % 16)),
-                pl.BlockSpec((16, 128), lambda s, k, owner: (0, 0)),
-            ],
-            out_specs=pl.BlockSpec((4, 8, 16, PW), lambda s, k, owner: (s, 0, 0, k)),
-            scratch_shapes=[pltpu.VMEM((PW, PW), jnp.bfloat16)],
-        ),
+        in_specs=[
+            pl.BlockSpec(memory_space=pltpu.SMEM),
+            pl.BlockSpec(memory_space=pl.ANY),
+            pl.BlockSpec(memory_space=pltpu.VMEM),
+        ],
+        out_specs=pl.BlockSpec(memory_space=pl.ANY),
+        scratch_shapes=[
+            pltpu.VMEM((PW, PW), jnp.bfloat16),
+            pltpu.VMEM((4, PW, PW), jnp.bfloat16),
+            pltpu.VMEM((4, 4, 8, 16, PW), jnp.bfloat16),
+            pltpu.SemaphoreType.DMA((4,)),
+            pltpu.SemaphoreType.DMA((4,)),
+        ],
     )(owner, interior, tile_mask)
+
+
+def hand_over_kernel(source, target, buffer, in_sem, out_sem):
+    def move(t, inward):
+        rows = pl.ds((t % 4) * 8, 8)
+        if inward:
+            return pltpu.make_async_copy(source.at[t // 4, rows], buffer.at[t], in_sem.at[t])
+        return pltpu.make_async_copy(buffer.at[t], target.at[t // 4, rows], out_sem.at[t])
+
+    for t in range(CHUNKS):
+        move(t, True).start()
+    for t in range(CHUNKS):
+        move(t, True).wait()
+        move(t, False).start()
+    for t in range(CHUNKS):
+        move(t, False).wait()
+
+
+def hand_over(result):
+    return pl.pallas_call(
+        hand_over_kernel,
+        out_shape=jax.ShapeDtypeStruct(result.shape, result.dtype),
+        in_specs=[pl.BlockSpec(memory_space=pl.ANY)],
+        out_specs=pl.BlockSpec(memory_space=pl.ANY),
+        scratch_shapes=[
+            pltpu.VMEM((CHUNKS, 8, 2 * HALF), jnp.float32),
+            pltpu.SemaphoreType.DMA((CHUNKS,)),
+            pltpu.SemaphoreType.DMA((CHUNKS,)),
+        ],
+    )(result)
 
 
 def coded(values):
@@ -244,85 +299,88 @@
 
     def second(t):
         for g, (first, width, tiles) in enumerate(GROUPS):
+            size = TILES[g]
             mine = dims[orders[g][1]][0]
             for copy in sum_copy(0, g, t):
                 copy.wait_recv()
 
-            def total(which, here, g=g):
+            def total(which, here, g=g, size=size):
                 return keep[g][t, which, :, :, here] + rcv1[g][t, which, :, :, here].astype(jnp.int32).astype(
                     jnp.float32
-                ) * scr[g][0, t, :, here].reshape(1, 1, TILE)
-
-            def send(j, _, g=g, mine=mine):
-                here = pl.ds(pl.multiple_of(j * TILE, TILE), TILE)
-                codes, scale = coded(total(1 - mine, here).reshape(32, TILE))
-                snd2[g][t, :, :, here] = codes.reshape(2, 16, TILE)
+                ) * scr[g][0, t, :, here].reshape(1, 1, size)
+
+            def send(j, _, g=g, size=size, mine=mine):
+                here = pl.ds(pl.multiple_of(j * size, size), size)
+                codes, scale = coded(total(1 - mine, here).reshape(32, size))
+                snd2[g][t, :, :, here] = codes.reshape(2, 16, size)
                 scs[g][1, t, :, here] = scale
                 return 0
 
-            lax.fori_loop(0, width // TILE, send, 0)
+            lax.fori_loop(0, width // size, send, 0)
             launch(t, functools.partial(sum_copy, 1, g))
 
-            def hold(j, _, g=g, mine=mine):
-                here = pl.ds(pl.multiple_of(j * TILE, TILE), TILE)
+            def hold(j, _, g=g, size=size, mine=mine):
+                here = pl.ds(pl.multiple_of(j * size, size), size)
                 keep[g][t, mine, :, :, here] = total(mine, here)
                 return 0
 
-            lax.fori_loop(0, width // TILE, hold, 0)
+            lax.fori_loop(0, width // size, hold, 0)
 
     def third(t):
         for g, (first, width, tiles) in enumerate(GROUPS):
+            size = TILES[g]
             mine2, mine3 = dims[orders[g][1]][0], dims[orders[g][2]][0]
             for copy in sum_copy(1, g, t):
                 copy.wait_recv()
 
-            def total(which, here, g=g):
+            def total(which, here, g=g, size=size):
                 return keep[g][t, mine2, which, :, here] + rcv2[g][t, which, :, here].astype(jnp.int32).astype(
                     jnp.float32
                 ) * scr[g][1, t, :, here]
 
-            def send(j, _, g=g, mine3=mine3):
-                here = pl.ds(pl.multiple_of(j * TILE, TILE), TILE)
+            def send(j, _, g=g, size=size, mine3=mine3):
+                here = pl.ds(pl.multiple_of(j * size, size), size)
                 codes, scale = coded(total(1 - mine3, here))
                 snd3[g][t, :, here] = codes
                 scs[g][2, t, :, here] = scale
                 return 0
 
-            lax.fori_loop(0, width // TILE, send, 0)
+            lax.fori_loop(0, width // size, send, 0)
             launch(t, functools.partial(sum_copy, 2, g))
 
-            def hold(j, _, g=g, mine2=mine2, mine3=mine3):
-                here = pl.ds(pl.multiple_of(j * TILE, TILE), TILE)
+            def hold(j, _, g=g, size=size, mine2=mine2, mine3=mine3):
+                here = pl.ds(pl.multiple_of(j * size, size), size)
                 keep[g][t, mine2, mine3, :, here] = total(mine3, here)
                 return 0
 
-            lax.fori_loop(0, width // TILE, hold, 0)
+            lax.fori_loop(0, width // size, hold, 0)
 
     def fourth(t):
         step, rows = t // 4, pl.ds(pl.multiple_of((t % 4) * 8, 8), 8)
         for g, (first, width, tiles) in enumerate(GROUPS):
+            size = TILES[g]
             mine2, mine3 = dims[orders[g][1]][0], dims[orders[g][2]][0]
             for copy in sum_copy(2, g, t):
                 copy.wait_recv()
 
-            def finish(j, _, g=g, first=first, mine2=mine2, mine3=mine3):
-                here = pl.ds(pl.multiple_of(j * TILE, TILE), TILE)
+            def finish(j, _, g=g, size=size, first=first, mine2=mine2, mine3=mine3):
+                here = pl.ds(pl.multiple_of(j * size, size), size)
                 got = rcv3[g][t, :, here].astype(jnp.int32).astype(jnp.float32) * scr[g][2, t, :, here]
                 total = keep[g][t, mine2, mine3, :, here] + got
                 low, high = total[:8], total[8:]
                 snd4[g][t, :, here] = jnp.where(core == 0, high, low)
-                there = pl.ds(pl.multiple_of(core * HALF + first + j * TILE, TILE), TILE)
+                there = pl.ds(pl.multiple_of(core * HALF + first + j * size, size), size)
                 out_ref[step, rows, there] = out_ref[step, rows, there] - jnp.where(core == 0, low, high)
                 return 0
 
-            lax.fori_loop(0, width // TILE, finish, 0)
+            lax.fori_loop(0, width // size, finish, 0)
             launch(t, lambda t, g=g: [last_copy(g, t)])
 
     def fifth(t):
         step, rows = t // 4, pl.ds(pl.multiple_of((t % 4) * 8, 8), 8)
         for g, (first, width, tiles) in enumerate(GROUPS):
             last_copy(g, t).wait_recv()
-            there = pl.ds(pl.multiple_of((1 - core) * HALF + first, TILE), width)
+            there = pl.ds(pl.multiple_of((1 - core) * HALF + first, 128), width)
             out_ref[step, rows, there] = out_ref[step, rows, there] - rcv4[g][t]
         out_copy(t).start()
 
@@ -416,7 +474,7 @@
 
     f32, i16, bf16 = jnp.float32, jnp.int16, jnp.bfloat16
     dma = pltpu.SemaphoreType.DMA
-    return pl.pallas_call(
+    result = pl.pallas_call(
         main_kernel,
         out_shape=jax.ShapeDtypeStruct(stiffness.shape, f32),
         in_specs=[
@@ -458,6 +516,7 @@
             collective_id=0, has_side_effects=True, vmem_limit_bytes=62 * 1024 * 1024
         ),
     )(interior, tile_mask, cand, stiffness)
+    return hand_over(result)
 
 
 def solution(mesh):

time: 109 us -> 106 us (0.972)
  local copies, waits for them, and re-layouts: 3.06 us -> 0 us
    unnamed x1 -> x0, local copies, waits for them, and re-layouts: 3.06 us -> none
    pallas_call x0 -> x1, Pallas kernels: none -> 2.39 us  [hand_over(): pl.pallas_call(hand_over_kernel, out_shape=jax.ShapeDtypeStruct(result.sh...]
    pallas_call x1, Pallas kernels: 6.2 us -> 4.58 us  [pick(): pl.pallas_call(pick_kernel, out_shape=jax.ShapeDtypeStruct((CHUNKS, 8, 16...]
    pallas_call x1, Pallas kernels: 99.9 us -> 98.4 us  [shards(): pl.pallas_call(main_kernel, out_shape=jax.ShapeDtypeStruct(stiffness.shap...]
where the time goes in v3:
time: 106 us; the launch traced here: 105 us
  Pallas kernels  105 us (99%)
    pallas_call x1, Pallas kernels, shards(): pl.pallas_call(main_kernel, out_shape=jax.ShapeDtypeStruct(stiffness.shap...  98.4 us
    pallas_call x1, Pallas kernels, pick(): pl.pallas_call(pick_kernel, out_shape=jax.ShapeDtypeStruct((CHUNKS, 8, 16...  4.58 us
    pallas_call x1, Pallas kernels, hand_over(): pl.pallas_call(hand_over_kernel, out_shape=jax.ShapeDtypeStruct(result.sh...  2.39 us

profile of v3, /device:TPU:1, one launch (start us, length us, event | category | flops | bytes accessed | tf_op | source)
XLA Modules:
  0.0 105.4 jit_solution(17482199572009097569)
XLA Ops:
  0.0 4.6 %shard_map.46.cand = bf16[8,8,16,1024]{3,2,1,0:T(8,128)(2,1)} custom-call(s32[2]{0:T(128)} %owner_ref.1, bf16[1024,8192]{1,0:T(8,128)(2,1)} %w_hbm.3, s32[16,128]{1,0:T(8,128)} %mask_ref.3), custom_call_target="tpu_custom_call" | custom-call | tf_op jit(solution)/shard_map/pallas_call | solution.py:74
  4.6 98.4 %shard_map.47.source = f32[2,32,8192]{2,1,0:T(8,128)} custom-call(bf16[1024,8192]{1,0:T(8,128)(2,1)} %w_hbm.3, s32[16,128]{1,0:T(8,128)} %mask_ref.3, bf16[8,8,16,1024]{3,2,1,0:T(8,128)(2,1)} %shard_map.46.cand, f32[2,32,8192]{2,1,0:T(8,128)} %stiff_hbm.1), custom_call_target="tpu_custom_call" | custom-call | tf_op jit(solution)/shard_map/pallas_call | solution.py:477
  103.0 2.4 %shard_map.48 = f32[2,32,8192]{2,1,0:T(8,128)} custom-call(f32[2,32,8192]{2,1,0:T(8,128)} %shard_map.47.source), custom_call_target="tpu_custom_call" | custom-call | tf_op jit(solution)/shard_map/pallas_call | solution.py:110

commit v4 on v3

--- a/solution.py
+++ b/solution.py
@@ -12,6 +12,7 @@
 MESH = pl.DeviceIdType.MESH
 CHUNKS = 8
 SLOTS = 4
+SENDS = 2
 LAG = 4
 HALF = 4096
 DEPTH = 1024
@@ -185,31 +186,43 @@
     def quarter(z):
         return pl.ds(2 * z, 2)
 
-    def scatter(d, t):
-        return remote(cand.at[t, quarter(others[d])], r1.at[t, d], c1_s.at[d, t % SLOTS], c1_r.at[d, t % SLOTS], ring[d])
-
-    def cross(t):
-        return remote(s1.at[t], r2.at[t], c2_s.at[t % SLOTS], c2_r.at[t % SLOTS], across)
-
-    def gather(d, t):
-        piece = a.at[t, 0, quarter(z)]
-        return remote(piece, piece, c3_s.at[d, t % SLOTS], c3_r.at[d, t % SLOTS], ring[d])
-
-    def twin_a(t):
-        return remote(a.at[t, 0], a.at[t, 1], ac_s.at[t % SLOTS], ac_r.at[t % SLOTS], twin)
+    def piece(p):
+        return pl.ds(p * (DEPTH // 2), DEPTH // 2)
+
+    def scatter(p, d, t):
+        return remote(
+            cand.at[t, quarter(others[d]), :, piece(p)], r1.at[t, d, :, :, piece(p)],
+            c1_s.at[p, d, t % SENDS], c1_r.at[p, d, t % SLOTS], ring[d],
+        )
+
+    def cross(p, t):
+        return remote(
+            s1.at[t, :, :, piece(p)], r2.at[t, :, :, piece(p)],
+            c2_s.at[p, t % SENDS], c2_r.at[p, t % SLOTS], across,
+        )
+
+    def gather(p, d, t):
+        part = a.at[t, 0, quarter(z), :, piece(p)]
+        return remote(part, part, c3_s.at[p, d, t % SENDS], c3_r.at[p, d, t % SLOTS], ring[d])
+
+    def twin_a(p, t):
+        return remote(
+            a.at[t, 0, :, :, piece(p)], a.at[t, 1, :, :, piece(p)],
+            ac_s.at[p, t % SENDS], ac_r.at[p, t % SLOTS], twin,
+        )
 
     def sum_copy(stage, g, t):
         src = (snd1, snd2, snd3)[stage][g]
         dst = (rcv1, rcv2, rcv3)[stage][g]
         peer = dims[orders[g][stage]][1]
-        slot = t % SLOTS
+        slot, sent = t % SLOTS, t % SENDS
         return (
-            remote(src.at[t], dst.at[t], rd_s.at[stage, g, slot], rd_r.at[stage, g, slot], peer),
-            remote(scs[g].at[stage, t], scr[g].at[stage, t], rs_s.at[stage, g, slot], rs_r.at[stage, g, slot], peer),
+            remote(src.at[t], dst.at[t], rd_s.at[stage, g, sent], rd_r.at[stage, g, slot], peer),
+            remote(scs[g].at[stage, t], scr[g].at[stage, t], rs_s.at[stage, g, sent], rs_r.at[stage, g, slot], peer),
         )
 
     def last_copy(g, t):
-        return remote(snd4[g].at[t], rcv4[g].at[t], o_s.at[g, t % SLOTS], o_r.at[g, t % SLOTS], twin)
+        return remote(snd4[g].at[t], rcv4[g].at[t], o_s.at[g, t % SENDS], o_r.at[g, t % SLOTS], twin)
 
     mine_copy.start()
     for i in range(4):
@@ -218,38 +231,46 @@
     mask_copy.start()
 
     def launch(t, copies):
-        @pl.when(t >= SLOTS)
-        def _():
-            for copy in copies(t - SLOTS):
+        @pl.when(t >= SENDS)
+        def _():
+            for copy in copies(t - SENDS):
                 copy.wait_send()
 
         for copy in copies(t):
             copy.start()
 
-    def scatters(t):
-        return [scatter(d, t) for d in range(3)]
-
-    def gathers(t):
-        return [gather(d, t) for d in range(3)]
+    def scatters(p, t):
+        return [scatter(p, d, t) for d in range(3)]
+
+    def gathers(p, t):
+        return [gather(p, d, t) for d in range(3)]
 
     def spread_0(t):
-        launch(t, scatters)
+        for p in range(2):
+            launch(t, functools.partial(scatters, p))
 
     def spread_1(t):
-        for copy in scatters(t):
-            copy.wait_recv()
-        s1[t] = (mine_c[t] + r1[t, 0]) + (r1[t, 1] + r1[t, 2])
-        launch(t, lambda t: [cross(t)])
+        for p in range(2):
+            for copy in scatters(p, t):
+                copy.wait_recv()
+            cols = piece(p)
+            s1[t, :, :, cols] = (mine_c[t, :, :, cols] + r1[t, 0, :, :, cols]) + (
+                r1[t, 1, :, :, cols] + r1[t, 2, :, :, cols]
+            )
+            launch(t, lambda t, p=p: [cross(p, t)])
 
     def spread_2(t):
-        cross(t).wait_recv()
-        a[t, 0, quarter(z)] = s1[t] + r2[t]
-        launch(t, gathers)
+        for p in range(2):
+            cross(p, t).wait_recv()
+            cols = piece(p)
+            a[t, 0, quarter(z), :, cols] = s1[t, :, :, cols] + r2[t, :, :, cols]
+            launch(t, functools.partial(gathers, p))
 
     def spread_3(t):
-        for copy in gathers(t):
-            copy.wait_recv()
-        launch(t, lambda t: [twin_a(t)])
+        for p in range(2):
+            for copy in gathers(p, t):
+                copy.wait_recv()
+            launch(t, lambda t, p=p: [twin_a(p, t)])
 
     def mask_slice(half, ref, i):
         cols = pl.ds(pl.multiple_of(i * 1024, 1024), 1024)
@@ -265,7 +286,8 @@
                 b[row : row + 16, cols] = b[row : row + 16, cols] * factor
 
     def product(t):
-        twin_a(t).wait_recv()
+        for p in range(2):
+            twin_a(p, t).wait_recv()
         for g, (first, width, tiles) in enumerate(GROUPS):
             if g == 1:
 
@@ -405,17 +427,25 @@
             mine_copy.wait()
             mask_copy.wait_recv()
 
-        @pl.when(i < 2)
-        def _():
-            for j in range(2):
-                local_b(2 * i + j).wait()
-                mask_slice(0, mask_ref, 2 * i + j)
-
-        @pl.when(i == 3)
-        def _():
-            for j in range(2):
-                remote_b(j).wait_recv()
-                mask_slice(1, mask2, j)
+        def own_slice(j):
+            local_b(j).wait()
+            mask_slice(0, mask_ref, j)
+
+        def other_slice(j):
+            remote_b(j).wait_recv()
+            mask_slice(1, mask2, j)
+
+        @pl.when(i < 3)
+        def _():
+            own_slice(i)
+
+        @pl.when(i == 0)
+        def _():
+            own_slice(3)
+
+        @pl.when((i >= 2) & (i < 4))
+        def _():
+            other_slice(i - 2)
 
         during(LAG, product)
 
@@ -453,16 +483,14 @@
             for g in range(3):
                 for copy in sum_copy(stage, g, t):
                     copy.wait_send()
-        for d in range(3):
-            scatter(d, t).wait_send()
-            gather(d, t).wait_send()
-        cross(t).wait_send()
-        twin_a(t).wait_send()
+        for p in range(2):
+            for copy in (*scatters(p, t), *gathers(p, t), cross(p, t), twin_a(p, t)):
+                copy.wait_send()
         for g in range(3):
             last_copy(g, t).wait_send()
         return 0
 
-    lax.fori_loop(CHUNKS - SLOTS, CHUNKS, drain, 0)
+    lax.fori_loop(CHUNKS - SENDS, CHUNKS, drain, 0)
 
 
 def shards(interior, tile_mask, owner, stiffness):
@@ -504,11 +532,11 @@
             each(f32, CHUNKS, 8),
             each(f32, 3, CHUNKS, 1),
             each(f32, 3, CHUNKS, 1),
-            dma((3, SLOTS)), dma((3, SLOTS)), dma((SLOTS,)), dma((SLOTS,)), dma((3, SLOTS)), dma((3, SLOTS)),
-            dma((SLOTS,)), dma((SLOTS,)),
-            dma((3, 3, SLOTS)), dma((3, 3, SLOTS)),
-            dma((3, 3, SLOTS)), dma((3, 3, SLOTS)),
-            dma((3, SLOTS)), dma((3, SLOTS)),
+            dma((2, 3, SENDS)), dma((2, 3, SLOTS)), dma((2, SENDS)), dma((2, SLOTS)),
+            dma((2, 3, SENDS)), dma((2, 3, SLOTS)), dma((2, SENDS)), dma((2, SLOTS)),
+            dma((3, 3, SENDS)), dma((3, 3, SLOTS)),
+            dma((3, 3, SENDS)), dma((3, 3, SLOTS)),
+            dma((3, SENDS)), dma((3, SLOTS)),
             dma((4,)), dma((4,)), dma((4,)),
             dma((1,)), dma((1,)), dma((1,)), dma((1,)), dma((CHUNKS,)),
         ],

time: 106 us -> 104 us (0.981)
    pallas_call x1, Pallas kernels: 98.4 us -> 96.7 us  [shards(): pl.pallas_call(main_kernel, out_shape=jax.ShapeDtypeStruct(stiffness.shap...]
where the time goes in v4:
time: 104 us
  Pallas kernels  104 us (100%)
    pallas_call x1, Pallas kernels, shards(): pl.pallas_call(main_kernel, out_shape=jax.ShapeDtypeStruct(stiffness.shap...  96.7 us
    pallas_call x1, Pallas kernels, pick(): pl.pallas_call(pick_kernel, out_shape=jax.ShapeDtypeStruct((CHUNKS, 8, 16...  4.58 us
    pallas_call x1, Pallas kernels, hand_over(): pl.pallas_call(hand_over_kernel, out_shape=jax.ShapeDtypeStruct(result.sh...  2.39 us

profile of v4, /device:TPU:1, one launch (start us, length us, event | category | flops | bytes accessed | tf_op | source)
XLA Modules:
  0.0 103.7 jit_solution(7003988703500352810)
XLA Ops:
  0.0 4.6 %shard_map.46.cand = bf16[8,8,16,1024]{3,2,1,0:T(8,128)(2,1)} custom-call(s32[2]{0:T(128)} %owner_ref.1, bf16[1024,8192]{1,0:T(8,128)(2,1)} %w_hbm.3, s32[16,128]{1,0:T(8,128)} %mask_ref.3), custom_call_target="tpu_custom_call" | custom-call | tf_op jit(solution)/shard_map/pallas_call | solution.py:75
  4.6 96.7 %shard_map.47.source = f32[2,32,8192]{2,1,0:T(8,128)} custom-call(bf16[1024,8192]{1,0:T(8,128)(2,1)} %w_hbm.3, s32[16,128]{1,0:T(8,128)} %mask_ref.3, bf16[8,8,16,1024]{3,2,1,0:T(8,128)(2,1)} %shard_map.46.cand, f32[2,32,8192]{2,1,0:T(8,128)} %stiff_hbm.1), custom_call_target="tpu_custom_call" | custom-call | tf_op jit(solution)/shard_map/pallas_call | solution.py:505
  101.3 2.4 %shard_map.48 = f32[2,32,8192]{2,1,0:T(8,128)} custom-call(f32[2,32,8192]{2,1,0:T(8,128)} %shard_map.47.source), custom_call_target="tpu_custom_call" | custom-call | tf_op jit(solution)/shard_map/pallas_call | solution.py:111

commit v5 on v4

--- a/solution.py
+++ b/solution.py
@@ -17,7 +17,7 @@
 HALF = 4096
 DEPTH = 1024
 GROUPS = ((0, 1792, (1024, 768)), (1792, 1408, (768, 640)), (3200, 896, (896,)))
-TILES = (256, 128, 128)
+TILES = (896, 1408, 896)
 
 
 def pick_kernel(owner_ref, w_hbm, mask_ref, out_hbm, order, blocks, turned, in_sem, out_sem):
@@ -319,6 +319,10 @@
                 done += size
             launch(t, functools.partial(sum_copy, 0, g))
 
+    def sweep(count, body):
+        for j in range(count):
+            body(j)
+
     def second(t):
         for g, (first, width, tiles) in enumerate(GROUPS):
             size = TILES[g]
@@ -331,22 +335,22 @@
                     jnp.float32
                 ) * scr[g][0, t, :, here].reshape(1, 1, size)
 
-            def send(j, _, g=g, size=size, mine=mine):
-                here = pl.ds(pl.multiple_of(j * size, size), size)
+            def send(j, g=g, size=size, mine=mine):
+                here = pl.ds(j * size, size)
                 codes, scale = coded(total(1 - mine, here).reshape(32, size))
                 snd2[g][t, :, :, here] = codes.reshape(2, 16, size)
                 scs[g][1, t, :, here] = scale
                 return 0
 
-            lax.fori_loop(0, width // size, send, 0)
+            sweep(width // size, send)
             launch(t, functools.partial(sum_copy, 1, g))
 
-            def hold(j, _, g=g, size=size, mine=mine):
-                here = pl.ds(pl.multiple_of(j * size, size), size)
+            def hold(j, g=g, size=size, mine=mine):
+                here = pl.ds(j * size, size)
                 keep[g][t, mine, :, :, here] = total(mine, here)
                 return 0
 
-            lax.fori_loop(0, width // size, hold, 0)
+            sweep(width // size, hold)
 
     def third(t):
         for g, (first, width, tiles) in enumerate(GROUPS):
@@ -360,22 +364,22 @@
                     jnp.float32
                 ) * scr[g][1, t, :, here]
 
-            def send(j, _, g=g, size=size, mine3=mine3):
-                here = pl.ds(pl.multiple_of(j * size, size), size)
+            def send(j, g=g, size=size, mine3=mine3):
+                here = pl.ds(j * size, size)
                 codes, scale = coded(total(1 - mine3, here))
                 snd3[g][t, :, here] = codes
                 scs[g][2, t, :, here] = scale
                 return 0
 
-            lax.fori_loop(0, width // size, send, 0)
+            sweep(width // size, send)
             launch(t, functools.partial(sum_copy, 2, g))
 
-            def hold(j, _, g=g, size=size, mine2=mine2, mine3=mine3):
-                here = pl.ds(pl.multiple_of(j * size, size), size)
+            def hold(j, g=g, size=size, mine2=mine2, mine3=mine3):
+                here = pl.ds(j * size, size)
                 keep[g][t, mine2, mine3, :, here] = total(mine3, here)
                 return 0
 
-            lax.fori_loop(0, width // size, hold, 0)
+            sweep(width // size, hold)
 
     def fourth(t):
         step, rows = t // 4, pl.ds(pl.multiple_of((t % 4) * 8, 8), 8)
@@ -385,17 +389,17 @@
             for copy in sum_copy(2, g, t):
                 copy.wait_recv()
 
-            def finish(j, _, g=g, size=size, first=first, mine2=mine2, mine3=mine3):
-                here = pl.ds(pl.multiple_of(j * size, size), size)
+            def finish(j, g=g, size=size, first=first, mine2=mine2, mine3=mine3):
+                here = pl.ds(j * size, size)
                 got = rcv3[g][t, :, here].astype(jnp.int32).astype(jnp.float32) * scr[g][2, t, :, here]
                 total = keep[g][t, mine2, mine3, :, here] + got
                 low, high = total[:8], total[8:]
                 snd4[g][t, :, here] = jnp.where(core == 0, high, low)
-                there = pl.ds(pl.multiple_of(core * HALF + first + j * size, size), size)
+                there = pl.ds(pl.multiple_of(core * HALF + first + j * size, 128), size)
                 out_ref[step, rows, there] = out_ref[step, rows, there] - jnp.where(core == 0, low, high)
                 return 0
 
-            lax.fori_loop(0, width // size, finish, 0)
+            sweep(width // size, finish)
             launch(t, lambda t, g=g: [last_copy(g, t)])
 
     def fifth(t):

time: 104 us -> 103 us (level)
  no operation moved by 1% of the time
where the time goes in v5:
time: 103 us
  Pallas kernels  103 us (100%)
    pallas_call x1, Pallas kernels, shards(): pl.pallas_call(main_kernel, out_shape=jax.ShapeDtypeStruct(stiffness.shap...  95.9 us
    pallas_call x1, Pallas kernels, pick(): pl.pallas_call(pick_kernel, out_shape=jax.ShapeDtypeStruct((CHUNKS, 8, 16...  4.58 us
    pallas_call x1, Pallas kernels, hand_over(): pl.pallas_call(hand_over_kernel, out_shape=jax.ShapeDtypeStruct(result.sh...  2.39 us

profile of v5, /device:TPU:1, one launch (start us, length us, event | category | flops | bytes accessed | tf_op | source)
XLA Modules:
  0.0 102.9 jit_solution(16281890713103075892)
XLA Ops:
  0.0 4.6 %shard_map.46.cand = bf16[8,8,16,1024]{3,2,1,0:T(8,128)(2,1)} custom-call(s32[2]{0:T(128)} %owner_ref.1, bf16[1024,8192]{1,0:T(8,128)(2,1)} %w_hbm.3, s32[16,128]{1,0:T(8,128)} %mask_ref.3), custom_call_target="tpu_custom_call" | custom-call | tf_op jit(solution)/shard_map/pallas_call | solution.py:75
  4.6 95.9 %shard_map.47.source = f32[2,32,8192]{2,1,0:T(8,128)} custom-call(bf16[1024,8192]{1,0:T(8,128)(2,1)} %w_hbm.3, s32[16,128]{1,0:T(8,128)} %mask_ref.3, bf16[8,8,16,1024]{3,2,1,0:T(8,128)(2,1)} %shard_map.46.cand, f32[2,32,8192]{2,1,0:T(8,128)} %stiff_hbm.1), custom_call_target="tpu_custom_call" | custom-call | tf_op jit(solution)/shard_map/pallas_call | solution.py:509
  100.5 2.4 %shard_map.48 = f32[2,32,8192]{2,1,0:T(8,128)} custom-call(f32[2,32,8192]{2,1,0:T(8,128)} %shard_map.47.source), custom_call_target="tpu_custom_call" | custom-call | tf_op jit(solution)/shard_map/pallas_call | solution.py:111
